TPU v7x, 128 devices: a whole 4x4x4 slice. The times are simulated.
128 devices in a mesh: shard: 128 (over z, x, y, core).
Axes of the slice: x: 4, y: 4, z: 4, core: 2. Of those that a mesh axis runs over, the one named last changes fastest.
Arguments:
- embeddings: bfloat16 [2048, 128, 1280], P('shard'), may hold values from -6 to 6
- lengths: int32 [2048], P('shard'), may hold values from 16 to 128
- requests: int32 [128, 128], P('shard'), may hold values from -1 to 15, as said below
- query_local: int32 [128, 128], P('shard'), may hold values from 0 to 15
Outputs:
- local_best: float32 [2048, 128], P('shard')
- cross_best: float32 [2048, 128], P('shard')
Inputs may be any that keep to these rules, and one draw needn't show every extreme that they name: requests[d, o] is -1 where cluster d lists no partner in cluster o, else a protein index within cluster o; requests[d, d] is -1; the number of listed partners differs from cluster to cluster.
All inputs are finite; a program needn't handle non-finite values.
Results may differ from a plain program's by a relative error of at most 0.0003.
Values may be sent and summed in bfloat16 or wider, within the bound.
No kernel may reach another device: no remote copies, remote signals or barrier semaphores. Data moves between devices by JAX's collectives and lax.ppermute only.
A program may use at most 256 MiB of HBM per device.

v0:
```python
import jax
import jax.numpy as jnp
from jax import lax
from jax.sharding import PartitionSpec as P

lowest = -1e30


def centred(score_matrix, row_validity_mask, col_mask):
    row_count = jnp.sum(row_validity_mask, -1)
    col_count = jnp.sum(col_mask, -1)
    row_mean = jnp.sum(score_matrix * col_mask[..., None, :], -1) / col_count[..., None]
    col_mean = jnp.sum(score_matrix * row_validity_mask[..., :, None], -2) / row_count[..., None]
    grand_mean = jnp.sum(row_mean * row_validity_mask, -1) / row_count
    return (
        score_matrix - row_mean[..., :, None] - col_mean[..., None, :] + grand_mean[..., None, None]
    )


def pair_side_flags(
    query_embedding, partner_embedding, query_mask, partner_mask, is_live, inverse_square_root
):
    score_matrix = (
        jnp.einsum(
            "dzp,dwp->dzw", query_embedding, partner_embedding, preferred_element_type=jnp.float32
        )
        * inverse_square_root
    )
    cent = centred(score_matrix, query_mask, partner_mask)
    row_side = jnp.max(jnp.where(partner_mask[:, None, :] > 0, cent, lowest), -1)
    col_side = jnp.max(jnp.where(query_mask[:, :, None] > 0, cent, lowest), -2)
    row_side = jnp.where(is_live[:, None], row_side, lowest)
    col_side = jnp.where(is_live[:, None], col_side, lowest)
    return (row_side, col_side)


def merge_into(values, targets, is_live, proteins_here):
    targeted = (targets[None, :] == jnp.arange(proteins_here)[:, None]) & is_live[None, :]
    return jnp.max(jnp.where(targeted[:, :, None], values[None, :, :], lowest), 1)


def per_device(embeddings, lengths, requests, query_local):
    proteins_here, slots, width = embeddings.shape
    peer_count = lax.axis_size("shard")
    inverse_square_root = 1.0 / jnp.sqrt(jnp.float32(width))
    masks = (jnp.arange(slots)[None, :] < lengths[:, None]).astype(jnp.float32)
    block_size = 8
    block_count = proteins_here // block_size

    def one_block(block_start):
        block_rows = lax.dynamic_slice_in_dim(embeddings, block_start, block_size, 0)
        block_mask = lax.dynamic_slice_in_dim(masks, block_start, block_size, 0)
        score_matrix = (
            jnp.einsum("bie,qje->bqij", block_rows, embeddings, preferred_element_type=jnp.float32)
            * inverse_square_root
        )
        cent = centred(score_matrix, block_mask[:, None, :], masks[None, :, :])
        row_max = jnp.max(jnp.where(masks[None, :, None, :] > 0, cent, lowest), -1)
        self_pair = (block_start + jnp.arange(block_size))[:, None] == jnp.arange(proteins_here)[
            None, :
        ]
        row_max = jnp.where(self_pair[:, :, None], lowest, row_max)
        best_match = jnp.max(row_max, 1)
        return jnp.where(block_mask > 0, best_match, 0.0)

    start_offsets = jnp.arange(block_count) * block_size
    local_best = lax.map(one_block, start_offsets).reshape(proteins_here, slots)
    wanted = requests[0]
    query_pick = query_local[0]
    listed = wanted >= 0
    asked_slot = lax.all_to_all(wanted[:, None], "shard", split_axis=0, concat_axis=0, tiled=True)[
        :, 0
    ]
    asked_live = asked_slot >= 0
    asked_index = jnp.clip(asked_slot, 0)
    sent_rows = embeddings[asked_index]
    arrived = lax.all_to_all(sent_rows, "shard", split_axis=0, concat_axis=0, tiled=True)
    every_length = lax.all_gather(lengths, "shard", axis=0, tiled=True)
    owner_ids = jnp.arange(peer_count) * proteins_here + jnp.clip(wanted, 0)
    partner_len = every_length[owner_ids]
    partner_mask = (jnp.arange(slots)[None, :] < partner_len[:, None]).astype(jnp.float32)
    query_embedding = embeddings[query_pick]
    query_mask = masks[query_pick]
    row_side, col_side = pair_side_flags(
        query_embedding, arrived, query_mask, partner_mask, listed, inverse_square_root
    )
    returned = lax.all_to_all(col_side, "shard", split_axis=0, concat_axis=0, tiled=True)
    from_rows = merge_into(row_side, query_pick, listed, proteins_here)
    from_cols = merge_into(returned, asked_index, asked_live, proteins_here)
    best = jnp.maximum(from_rows, from_cols)
    cross_best = jnp.where((masks > 0) & (best > -1e29), best, 0.0)
    return (local_best, cross_best)


def solution(mesh):
    placed = (P("shard", None, None), P("shard"), P("shard", None), P("shard", None))
    return jax.shard_map(
        per_device,
        mesh=mesh,
        in_specs=placed,
        out_specs=(P("shard", None), P("shard", None)),
        check_vma=False,
    )
```

profile of v0, /device:TPU:1, one launch (start us, length us, event | category | flops | bytes accessed | tf_op | source)
XLA Modules:
  0.0 847.1 jit_solution(16752613588207237252)
XLA Ops:
  0.6 0.8 copy.8
  1.4 20.9 %all_to_all.20 = s32[128,1,1]{2,1,0:T(1,128)S(1)} all-to-all(s32[128,1,1]{2,1,0:T(1,128)S(1)} %copy.8), channel_id=1, replica_groups=mesh['shard'=128] {'shard'}, dimensions={0} | all-to-all | bytes 1024 | tf_op jit(solution)/shard_map/all_to_all | solution.py:71
  22.3 2.4 maximum_reduce_fusion
  24.7 17.7 %gather_fusion.2 = bf16[128,128,1280]{2,1,0:T(8,128)(2,1)} fusion(bf16[16,128,1280]{2,1,0:T(8,128)(2,1)} %param.6, s32[1024]{0:T(1024)S(1)} %pad_clamp_fusion), kind=kCustom, calls=%fused_computation.2 | custom fusion | bytes 83886592 | tf_op jit(solution)/shard_map/gather | solution.py:76
  42.3 5.7 all-to-all-start.1
  48.1 17.9 %gather_fusion.1 = bf16[128,128,1280]{2,1,0:T(8,128)(2,1)} fusion(bf16[16,128,1280]{2,1,0:T(8,128)(2,1)} %param.6, s32[1024]{0:T(1024)S(1)} %pad_clamp_fusion.1), kind=kCustom, calls=%fused_computation.1 | custom fusion | bytes 83886592 | tf_op jit(solution)/shard_map/gather | solution.py:82
  67.0 683.9 %all-reduce = s32[2048]{0:T(1024)S(1)} all-reduce(s32[2048]{0:T(1024)S(1)} %dynamic-update-slice), channel_id=1, replica_groups=mesh['shard'=128] {'shard'}, use_global_device_ids=true, to_apply=%add | all-reduce | flops 2048 | bytes 16384
  750.9 1.1 gather_fusion
  752.4 2.4 compare_reduce_fusion
  754.8 31.2 %multiply_reduce_fusion.3 = (f32[128,128]{1,0:T(8,128)S(1)}, f32[128,128]{1,0:T(8,128)S(1)}, f32[128,128,128]{2,1,0:T(8,128)}) fusion(f32[128,128]{1,0:T(8,128)S(1)} %get-tuple-element.87, f32[128,128]{1,0:T(8,128)S(1)} %get-tuple-element.85, bf16[128,128,1280]{2,1,0:T(8,128)(2,1)} %gather_fusion.1, bf16[128,128,1280]{2,1,0:T(8,128)(2,1)} %all-to-all-done.1), kind=kOutput, calls=%fused_computation.31 | convolution fusion | flops 5377064960 | bytes 92536832 | tf_op jit(solution)/shard_map/dzp,dwp->dzw/dot_general | solution.py:24
  786.3 9.6 %select_reduce_fusion.1 = (f32[128,128]{1,0:T(8,128)S(1)}, f32[128,128]{1,0:T(8,128)S(1)}) fusion(f32[128,128,128]{2,1,0:T(8,128)} %get-tuple-element.86, f32[128]{0:T(128)S(1)} %div.79, f32[128,128]{1,0:T(8,128)S(1)} %broadcast_divide_fusion.2, f32[128,128]{1,0:T(8,128)S(1)} %get-tuple-element.79, pred[128,128]{1,0:T(8,128)(4,1)S(1)} %broadcast_compare_fusion.1, ...), kind=kLoop, calls=%fused_computation.28 | loop fusion | flops 16744448 | bytes 8684032 | tf_op jit(solution)/shard_map/reduce_max | solution.py:31
  795.8 0.8 broadcast_select_fusion
  796.7 5.3 all-to-all-start.2
  802.4 9.3 %all-to-all-done.2 = f32[128,1,128]{2,1,0:T(1,128)S(1)} async-done(((f32[128,1,128]{2,1,0:T(1,128)}), f32[128,1,128]{2,1,0:T(1,128)S(1)}, u32[]{:S(2)}, u32[]{:S(2)}) %all-to-all-start.2) | async-done | bytes 65568 | tf_op jit(solution)/shard_map/all_to_all | solution.py:87
  812.0 0.8 and_select_fusion
  812.8 33.8 %while.11 = (s32[]{:T(128)}, f32[2,8,128]{2,1,0:T(8,128)S(1)}, s32[2]{0:T(128)S(1)}, f32[16,128]{1,0:T(8,128)S(1)}, bf16[16,128,1280]{2,1,0:T(8,128)(2,1)}, /*in...) while((s32[]{:T(128)}, f32[2,8,128]{2,1,0:T(8,128)S(1)}, s32[2]{0:T(128)S(1)}, f32[16,128]{1,0:T(8,128)S(1)}, ...), condition=%wide.region_8.9_spmd, body=%wide.region_1.8_spmd.sunk | while | flops 5389736960 | bytes 25377412 | solution.py:67
  812.8 0.7 dynamic_slice.24
  815.5 0.7 iota_add_fusion.2
  816.4 9.8 %multiply_reduce_fusion.8 = (f32[8,16,128]{2,1,0:T(8,128)S(1)}, f32[8,128,16]{1,2,0:T(8,128)S(1)}, f32[8,128,16,128]{1,3,2,0:T(8,128)S(1)}) fusion(f32[8,128]{1,0:T(8,128)S(1)} %broadcast_multiply_fusion.5, f32[16,128]{1,0:T(8,128)S(1)} %broadcast_multiply_fusion.6, bf16[16,128,1280]{2,1,0:T(8,128)(2,1)} %get-tuple-element.163, s32[]{:T(128)S(6)} %select_n.113), kind=kOutput, calls=%fused_computation.9.clone.1 | convolution fusion | flops 5377064960 | bytes 16396292 | tf_op jit(solution)/shard_map/while/body/eval_jaxpr/bie,qje->bqij/dot_general | solution.py:54
  826.5 3.3 fusion.23
  830.0 0.7 dynamic_slice.24
  832.7 0.7 iota_add_fusion.2
  833.6 9.2 %multiply_reduce_fusion.8 = (f32[8,16,128]{2,1,0:T(8,128)S(1)}, f32[8,128,16]{1,2,0:T(8,128)S(1)}, f32[8,128,16,128]{1,3,2,0:T(8,128)S(1)}) fusion(f32[8,128]{1,0:T(8,128)S(1)} %broadcast_multiply_fusion.5, f32[16,128]{1,0:T(8,128)S(1)} %broadcast_multiply_fusion.6, bf16[16,128,1280]{2,1,0:T(8,128)(2,1)} %get-tuple-element.163, s32[]{:T(128)S(6)} %select_n.113), kind=kOutput, calls=%fused_computation.9.clone.1 | convolution fusion | flops 5377064960 | bytes 16396292 | tf_op jit(solution)/shard_map/while/body/eval_jaxpr/bie,qje->bqij/dot_general | solution.py:54
  843.1 3.3 fusion.23
  (50 shorter events, 4.1 us)
Async XLA Ops:
  42.3 5.7 copy-start.2
  42.3 712.5 %all-to-all-start.1 = ((bf16[128,128,1280]{2,1,0:T(8,128)(2,1)}), bf16[128,128,1280]{2,1,0:T(8,128)(2,1)}, u32[]{:S(2)}, u32[]{:S(2)}) async-start(bf16[128,128,1280]{2,1,0:T(8,128)(2,1)} %gather_fusion.2), calls=%async_computation.1 | async-start | bytes 83886080 | tf_op jit(solution)/shard_map/all_to_all | solution.py:77
  48.1 17.9 %copy-start = (s32[16]{0:T(128)S(1)}, s32[16]{0:T(128)}, u32[]{:S(2)}) copy-start(s32[16]{0:T(128)} %param.7) | copy-start | bytes 196
  48.1 702.8 %copy-start.1 = (s32[1,128]{1,0:T(1,128)S(1)}, s32[1,128]{1,0:T(1,128)}, u32[]{:S(2)}) copy-start(s32[1,128]{1,0:T(1,128)} %param.8) | copy-start | bytes 1540
  796.7 14.9 %all-to-all-start.2 = ((f32[128,1,128]{2,1,0:T(1,128)}), f32[128,1,128]{2,1,0:T(1,128)S(1)}, u32[]{:S(2)}, u32[]{:S(2)}) async-start(f32[128,1,128]{2,1,0:T(1,128)} %broadcast_select_fusion), calls=%async_computation.2 | async-start | bytes 131072 | tf_op jit(solution)/shard_map/all_to_all | solution.py:87
  846.5 0.6 copy-start.3
where the time goes:
time: 848 us; the launch traced here: 847 us
  blocking collectives  705 us (83%)
  matrix products  50.2 us (6%)
  local copies, waits for them, and re-layouts  40.3 us (5%)
  other arithmetic  26.5 us (3%)
  starting transfers between devices  11 us (1%)
  waiting for transfers between devices  9.26 us (1%)
    unnamed x1, blocking collectives  684 us
    dot_general x1, matrix products, pair_side_flags(): jnp.einsum('dzp,dwp->dzw', query_embedding, partner_embedding, preferred_...  31.2 us
    all_to_all x1, blocking collectives, per_device(): lax.all_to_all(wanted[:, None], 'shard', split_axis=0, concat_axis=0, til...  20.9 us
    dot_general x2, matrix products, one_block(): jnp.einsum('bie,qje->bqij', block_rows, embeddings, preferred_element_typ...  19 us
    gather x1, local copies, waits for them, and re-layouts, per_device(): query_embedding = embeddings[query_pick]  17.9 us
    gather x1, local copies, waits for them, and re-layouts, per_device(): sent_rows = embeddings[asked_index]  17.7 us
  transfers between devices with their start and end apart: 2, of which 1 were waited for; matrix products, arithmetic and copies ran while one was open for 3% of the time, Pallas kernels for 0%

commit v1 on v0

v1 whole, which is shorter than its diff:
```python
import functools

import jax
import jax.numpy as jnp
from jax import lax
from jax.experimental import pallas as pl
from jax.experimental.pallas import tpu as pltpu
from jax.sharding import PartitionSpec as P

lowest = -1e30
N = 128
GR = 8
C1 = 2

R_F1ROW, R_F1COL, R_F2ROW, R_F2COL, R_SEND, R_SENDM, R_GIN, R_LIN, R_OWN, R_LEFT, R_GOUT = range(11)


def swap_rows(x, s):
    return jnp.where((s & 1) == 0, pltpu.roll(x, N - 1, 0), pltpu.roll(x, 1, 0))


def skew(x, by, axis, sign):
    for b in range(7):
        shift = (1 << b) if sign > 0 else N - (1 << b)
        x = jnp.where(((by >> b) & 1) == 1, pltpu.roll(x, shift, axis), x)
    return x


def route_kernel(c2, me_ref, req_ref, q_ref, lens_ref, lens_t_ref, tab_ref, tmp_ref):
    s = lax.broadcasted_iota(jnp.int32, (N, N), 0)
    r = lax.broadcasted_iota(jnp.int32, (N, N), 1)
    req = req_ref[...]
    q = q_ref[...]
    live = (req >= 0).astype(jnp.int32)
    req = jnp.maximum(req, 0)
    la = jnp.zeros((N, N), jnp.int32)
    lb = jnp.zeros((N, N), jnp.int32)
    for p in range(16):
        la = jnp.where(q == p, lens_ref[:, p : p + 1], la)
        lb = jnp.where(req == p, lens_t_ref[p : p + 1, :], lb)
    la = la * live
    lb = lb * live
    live_t = live.T
    both = live + live_t
    w_col = jnp.sum(both, axis=1, keepdims=True)
    w_row = jnp.sum(both, axis=0, keepdims=True)
    diff = ((lb + 15) >> 4) - ((la + 15) >> 4)
    score = (
        100 * (diff + diff.T)
        + (live - live_t) * (w_col - w_row)
        + jnp.where(((s + r) & 1) == 0, 25, -25)
    )
    lister_gets = score < 0
    lin = jnp.where(lister_gets, lb.T, la)
    psend = jnp.where(lister_gets, req.T, q)
    pown = jnp.where(lister_gets, q.T, req)
    m_tot = (lin + 15) >> 4

    diag = s == r
    m_sw = swap_rows(m_tot, s)
    free = jnp.where(diag, 0, C1)
    n_own = jnp.minimum(m_tot, free)
    rem = m_tot - n_own
    rem_sw = swap_rows(rem, s)
    n_mate = jnp.minimum(rem_sw, free - n_own)
    g_mate = m_sw - rem_sw
    w1 = free - n_own - n_mate
    for k in range(C1):
        own_code = (r << 3) | k
        mate_code = (1 << 10) | (r << 3) | (g_mate + k - n_own)
        code = jnp.where(k < n_own, own_code, jnp.where(k < n_own + n_mate, mate_code, 0))
        w1 = w1 | (code << (2 + 11 * k))
    rem = swap_rows(rem_sw - n_mate, s)
    free = jnp.where(diag, 0, c2)
    g_own = m_tot - rem
    n_own = jnp.minimum(rem, free)
    rem = rem - n_own
    rem_sw = swap_rows(rem, s)
    n_mate = jnp.minimum(rem_sw, free - n_own)
    g_mate = m_sw - rem_sw
    w2 = free - n_own - n_mate
    for k in range(c2):
        own_code = (g_own + k) << 2
        mate_code = 1 | ((g_mate + k - n_own) << 2)
        code = jnp.where(k < n_own, own_code, jnp.where(k < n_own + n_mate, mate_code, 0))
        w2 = w2 | (code << (2 + 14 * k))
    rem = swap_rows(rem_sw - n_mate, s)

    w1 = skew(w1, s, 1, -1)
    w2 = skew(w2, r, 0, -1)

    def sweep(flag, total, w1, w2, rem):
        def step(w1, w2, rem):
            f1 = w1 & 3
            f2 = w2 & 3
            ok = jnp.minimum(jnp.minimum(f1, f2), rem) > 0
            g = total - rem
            code1 = (flag << 10) | (r << 3) | g
            code2 = 2 | (g << 2) | ((C1 - f1) << 5) | (s << 6) | (flag << 13)
            new1 = (w1 - 1) | (code1 << jnp.where(f1 == C1, 2, 13))
            new2 = (w2 - 1) | (code2 << jnp.where(f2 == c2, 2, 16))
            w1 = jnp.where(ok, new1, w1)
            w2 = jnp.where(ok, new2, w2)
            rem = jnp.where(ok, rem - 1, rem)
            return pltpu.roll(w1, N - 1, 1), pltpu.roll(w2, N - 1, 0), rem

        def body(c):
            i, left, w1, w2, rem = c
            for _ in range(8):
                w1, w2, rem = step(w1, w2, rem)
            return i + 1, jnp.sum(rem), w1, w2, rem

        i, left, w1, w2, rem = lax.while_loop(
            lambda c: (c[0] < N // 8) & (c[1] > 0),
            body,
            (jnp.int32(0), jnp.sum(rem), w1, w2, rem),
        )
        return 8 * i, left, w1, w2, rem

    t_a, _, w1, w2, rem = sweep(0, m_tot, w1, w2, rem)
    t_b, left, w1, w2, rem = sweep(1, m_sw, w1, w2, swap_rows(rem, s))
    turn = (t_a + t_b) & (N - 1)
    w1 = skew(pltpu.roll(w1, turn, 1), s, 1, 1)
    w2 = skew(pltpu.roll(w2, turn, 0), r, 0, 1)

    me = me_ref[0]
    mate = me ^ 1

    def put(row, x, at):
        tmp_ref[...] = x
        tab_ref[row : row + 1, :] = tmp_ref[pl.ds(at, 1), :]

    put(R_F1ROW, w1, me)
    put(R_F1COL, w1.T, me)
    put(R_F2ROW, w2, me)
    put(R_F2COL, w2.T, me)
    put(R_SEND, psend, me)
    put(R_SENDM, psend, mate)
    put(R_GIN, m_tot.T, me)
    put(R_LIN, lin.T, me)
    put(R_OWN, pown.T, me)
    tab_ref[R_LEFT : R_LEFT + 1, :] = jnp.full((1, N), left, jnp.int32)
    put(R_GOUT, m_tot, me)
    tab_ref[R_GOUT + 1 :, :] = jnp.zeros((16 - R_GOUT - 1, N), jnp.int32)


def route(c2, me, req, q, lens):
    return pl.pallas_call(
        functools.partial(route_kernel, c2),
        out_shape=jax.ShapeDtypeStruct((16, N), jnp.int32),
        in_specs=[pl.BlockSpec(memory_space=pltpu.SMEM)] + [pl.BlockSpec(memory_space=pltpu.VMEM)] * 4,
        out_specs=pl.BlockSpec(memory_space=pltpu.VMEM),
        scratch_shapes=[pltpu.VMEM((N, N), jnp.int32)],
        compiler_params=pltpu.CompilerParams(vmem_limit_bytes=32 << 20),
        name=f"route{c2}",
    )(me, req, q, lens, lens.T)


def pack1_kernel(tab_ref, own_ref, mate_ref, out_ref, sem):
    def body(m, _):
        w = tab_ref[R_F1ROW, m]
        for k in range(C1):
            code = w >> (2 + 11 * k)
            g = code & 7
            to = (code >> 3) & (N - 1)
            from_mate = (code >> 10) & 1

            @pl.when(from_mate == 0)
            def _():
                at = tab_ref[R_SEND, to] * GR + g
                pltpu.make_async_copy(own_ref.at[at], out_ref.at[m * C1 + k], sem).start()

            @pl.when(from_mate == 1)
            def _():
                at = tab_ref[R_SENDM, to] * GR + g
                pltpu.make_async_copy(mate_ref.at[at], out_ref.at[m * C1 + k], sem).start()

        return 0

    lax.fori_loop(0, N, body, 0, unroll=4)
    pltpu.make_async_copy(out_ref, out_ref, sem).wait()


def pack2_kernel(c2, tab_ref, own_ref, mate_ref, got_ref, out_ref, sem):
    def body(to, _):
        w = tab_ref[R_F2ROW, to]
        for k in range(c2):
            code = w >> (2 + 14 * k)
            kind = code & 3
            g = (code >> 2) & 7
            slot = ((code >> 6) & (N - 1)) * C1 + ((code >> 5) & 1)
            dst = out_ref.at[to * c2 + k]

            @pl.when(kind == 0)
            def _():
                pltpu.make_async_copy(own_ref.at[tab_ref[R_SEND, to] * GR + g], dst, sem).start()

            @pl.when(kind == 1)
            def _():
                pltpu.make_async_copy(mate_ref.at[tab_ref[R_SENDM, to] * GR + g], dst, sem).start()

            @pl.when(kind >= 2)
            def _():
                pltpu.make_async_copy(got_ref.at[slot], dst, sem).start()

        return 0

    lax.fori_loop(0, N, body, 0, unroll=4)
    pltpu.make_async_copy(out_ref, out_ref, sem).wait()


def pack_whole_kernel(tab_ref, own_ref, out_ref, sem):
    def body(m, _):
        at = tab_ref[R_SEND, m] * GR
        pltpu.make_async_copy(own_ref.at[pl.ds(at, GR)], out_ref.at[pl.ds(m * GR, GR)], sem).start()
        return 0

    lax.fori_loop(0, N, body, 0)
    pltpu.make_async_copy(out_ref, out_ref, sem).wait()


def pack(kernel, slots, tab, *arrays):
    return pl.pallas_call(
        kernel,
        out_shape=jax.ShapeDtypeStruct((slots,) + arrays[0].shape[1:], arrays[0].dtype),
        in_specs=[pl.BlockSpec(memory_space=pltpu.SMEM)]
        + [pl.BlockSpec(memory_space=pl.ANY)] * len(arrays),
        out_specs=pl.BlockSpec(memory_space=pl.ANY),
        scratch_shapes=[pltpu.SemaphoreType.DMA],
    )(tab, *arrays)


def place_kernel(c2, me_ref, tab_ref, loc_ref):
    me = me_ref[0]

    def body(s, count):
        if c2 == 0:
            for g in range(GR):
                loc_ref[s * GR + g] = s * GR + g
        else:
            w = tab_ref[R_F1COL, s]
            filled = C1 - (w & 3)
            for k in range(C1):
                code = w >> (2 + 11 * k)

                @pl.when((k < filled) & (((code >> 3) & (N - 1)) == me))
                def _():
                    loc_ref[(s ^ ((code >> 10) & 1)) * GR + (code & 7)] = s * C1 + k

            w = tab_ref[R_F2COL, s]
            filled = c2 - (w & 3)
            for k in range(c2):
                code = w >> (2 + 14 * k)
                kind = code & 3
                via = ((code >> 6) & (N - 1)) ^ ((code >> 13) & 1)
                origin = jnp.where(kind >= 2, via, s ^ (kind & 1))

                @pl.when((k < filled) & (s != me))
                def _():
                    loc_ref[origin * GR + ((code >> 2) & 7)] = C1 * N + s * c2 + k

        is_live = tab_ref[R_GIN, s] > 0

        @pl.when(is_live)
        def _():
            loc_ref[N * GR + count] = s

        return count + is_live.astype(jnp.int32)

    loc_ref[N * GR + N] = lax.fori_loop(0, N, body, jnp.int32(0))


def place(c2, me, tab):
    return pl.pallas_call(
        functools.partial(place_kernel, c2),
        out_shape=jax.ShapeDtypeStruct((N * GR + N + 128,), jnp.int32),
        in_specs=[pl.BlockSpec(memory_space=pltpu.SMEM)] * 2,
        out_specs=pl.BlockSpec(memory_space=pltpu.SMEM),
    )(me, tab)


def match_kernel(n1, tab_ref, loc_ref, lens_ref, own_ref, got1_ref, got2_ref, best_ref, ret_ref, buf, sem):
    scale = 1.0 / jnp.sqrt(jnp.float32(own_ref.shape[2]))
    best_ref[...] = jnp.full(best_ref.shape, lowest, jnp.float32)
    ret_ref[...] = jnp.full(ret_ref.shape, lowest, jnp.float32)
    count = loc_ref[N * GR + N]

    def granules(i, act):
        s = loc_ref[N * GR + i]
        slot = i & 1
        for g in range(GR):

            @pl.when(g < tab_ref[R_GIN, s])
            def _():
                at = loc_ref[s * GR + g]

                @pl.when(at < n1)
                def _():
                    act(pltpu.make_async_copy(got1_ref.at[at], buf.at[slot, g], sem.at[slot, g]))

                @pl.when(at >= n1)
                def _():
                    act(pltpu.make_async_copy(got2_ref.at[at - n1], buf.at[slot, g], sem.at[slot, g]))

    @pl.when(count > 0)
    def _():
        granules(0, lambda c: c.start())

    row = lax.broadcasted_iota(jnp.int32, (N, N), 0)
    col = lax.broadcasted_iota(jnp.int32, (N, N), 1)

    def body(i, _):
        @pl.when(i + 1 < count)
        def _():
            granules(i + 1, lambda c: c.start())

        granules(i, lambda c: c.wait())
        s = loc_ref[N * GR + i]
        p = tab_ref[R_OWN, s]
        len_in = tab_ref[R_LIN, s]
        len_own = lens_ref[p]
        incoming = buf[i & 1].reshape(N, own_ref.shape[2])
        score = (
            lax.dot_general(
                own_ref[p], incoming, (((1,), (1,)), ((), ())), preferred_element_type=jnp.float32
            )
            * scale
        )
        real_in = col < len_in
        real_own = row < len_own
        over_in = jnp.sum(jnp.where(real_in, score, 0.0), 1, keepdims=True) / len_in.astype(jnp.float32)
        own_count = len_own.astype(jnp.float32)
        over_own = jnp.sum(jnp.where(real_own, score, 0.0), 0, keepdims=True) / own_count
        grand = jnp.sum(jnp.where(real_own[:, :1], over_in, 0.0), 0, keepdims=True) / own_count
        own_best = (
            jnp.max(jnp.where(real_in, score - over_own, lowest), 1, keepdims=True) - over_in + grand
        )
        in_best = (
            jnp.max(jnp.where(real_own, score - over_in, lowest), 0, keepdims=True) - over_own + grand
        )
        best = best_ref[...]
        best_ref[...] = jnp.where(col == p, jnp.maximum(best, own_best), best)
        ret_ref[pl.ds(s, 1), :] = in_best
        return 0

    lax.fori_loop(0, count, body, 0)


def match(n1, tab, loc, lens, own, got1, got2):
    return pl.pallas_call(
        functools.partial(match_kernel, n1),
        out_shape=[jax.ShapeDtypeStruct((N, N), jnp.float32)] * 2,
        in_specs=[pl.BlockSpec(memory_space=pltpu.SMEM)] * 3
        + [pl.BlockSpec(memory_space=pltpu.VMEM)]
        + [pl.BlockSpec(memory_space=pl.ANY)] * 2,
        out_specs=[pl.BlockSpec(memory_space=pltpu.VMEM)] * 2,
        scratch_shapes=[
            pltpu.VMEM((2, GR, 16, own.shape[2]), own.dtype),
            pltpu.SemaphoreType.DMA((2, GR)),
        ],
        compiler_params=pltpu.CompilerParams(vmem_limit_bytes=40 << 20),
        name="match",
    )(tab, loc, lens, own, got1, got2)


def centred(score_matrix, row_validity_mask, col_mask):
    row_count = jnp.sum(row_validity_mask, -1)
    col_count = jnp.sum(col_mask, -1)
    row_mean = jnp.sum(score_matrix * col_mask[..., None, :], -1) / col_count[..., None]
    col_mean = jnp.sum(score_matrix * row_validity_mask[..., :, None], -2) / row_count[..., None]
    grand_mean = jnp.sum(row_mean * row_validity_mask, -1) / row_count
    return (
        score_matrix - row_mean[..., :, None] - col_mean[..., None, :] + grand_mean[..., None, None]
    )


def within_cluster(embeddings, masks):
    proteins_here, slots, width = embeddings.shape
    inverse_square_root = 1.0 / jnp.sqrt(jnp.float32(width))
    block_size = 8
    block_count = proteins_here // block_size

    def one_block(block_start):
        block_rows = lax.dynamic_slice_in_dim(embeddings, block_start, block_size, 0)
        block_mask = lax.dynamic_slice_in_dim(masks, block_start, block_size, 0)
        score_matrix = (
            jnp.einsum("bie,qje->bqij", block_rows, embeddings, preferred_element_type=jnp.float32)
            * inverse_square_root
        )
        cent = centred(score_matrix, block_mask[:, None, :], masks[None, :, :])
        row_max = jnp.max(jnp.where(masks[None, :, None, :] > 0, cent, lowest), -1)
        self_pair = (block_start + jnp.arange(block_size))[:, None] == jnp.arange(proteins_here)[
            None, :
        ]
        row_max = jnp.where(self_pair[:, :, None], lowest, row_max)
        best_match = jnp.max(row_max, 1)
        return jnp.where(block_mask > 0, best_match, 0.0)

    start_offsets = jnp.arange(block_count) * block_size
    return lax.map(one_block, start_offsets).reshape(proteins_here, slots)


def exchange(x):
    return lax.all_to_all(x, "shard", split_axis=0, concat_axis=0, tiled=True)


def per_device(embeddings, lengths, requests, query_local):
    proteins_here, slots, width = embeddings.shape
    masks = (jnp.arange(slots)[None, :] < lengths[:, None]).astype(jnp.float32)
    me = lax.axis_index("shard").astype(jnp.int32)[None]
    mate_rows = lax.ppermute(embeddings, "shard", [(d, d ^ 1) for d in range(N)])
    plan = jnp.concatenate([requests, query_local, lengths[None, :]], 1)
    plan = lax.all_gather(plan, "shard", axis=0, tiled=True)
    req, q, lens = plan[:, :N], plan[:, N : 2 * N], plan[:, 2 * N :]
    own = embeddings.reshape(proteins_here * GR, 16, width)
    mate = mate_rows.reshape(proteins_here * GR, 16, width)

    def finish(tab, best, ret, local_best):
        returned = exchange(ret)
        mine = (tab[R_SEND][None, :] == jnp.arange(proteins_here)[:, None]) & (tab[R_GOUT] > 0)[None, :]
        from_ret = jnp.max(jnp.where(mine[:, :, None], returned[None, :, :], lowest), 1)
        best = jnp.maximum(from_ret, best[:, :proteins_here].T)
        cross_best = jnp.where((masks > 0) & (best > -1e29), best, 0.0)
        return local_best, cross_best

    def packed(c2, tab):
        loc = place(c2, me, tab)
        send1 = pack(pack1_kernel, N * C1, tab, own, mate)
        got1 = exchange(send1)
        local_best = within_cluster(embeddings, masks)
        got1, local_best = lax.optimization_barrier((got1, local_best))
        send2 = pack(functools.partial(pack2_kernel, c2), N * c2, tab, own, mate, got1)
        got2 = exchange(send2)
        best, ret = match(N * C1, tab, loc, lengths, embeddings, got1, got2)
        return finish(tab, best, ret, local_best)

    def whole(tab):
        loc = place(0, me, tab)
        got = exchange(pack(pack_whole_kernel, N * GR, tab, own))
        local_best = within_cluster(embeddings, masks)
        best, ret = match(N * GR, tab, loc, lengths, embeddings, got, got)
        return finish(tab, best, ret, local_best)

    def second(_):
        tab = route(2, me, req, q, lens)
        return lax.cond(tab[R_LEFT, 0] == 0, functools.partial(packed, 2), whole, tab)

    tab = route(1, me, req, q, lens)
    return lax.cond(tab[R_LEFT, 0] == 0, functools.partial(packed, 1), second, tab)


def solution(mesh):
    placed = (P("shard", None, None), P("shard"), P("shard", None), P("shard", None))
    return jax.shard_map(
        per_device,
        mesh=mesh,
        in_specs=placed,
        out_specs=(P("shard", None), P("shard", None)),
        check_vma=False,
    )
```

time: 848 us -> 801 us (0.945)
  blocking collectives: 705 us -> 37.3 us
  Pallas kernels: 0 us -> 519 us
  waiting for transfers between devices: 9.26 us -> 160 us
  local copies, waits for them, and re-layouts: 40.3 us -> 3.65 us
  starting transfers between devices: 11 us -> 42.4 us
  matrix products: 50.2 us -> 19.2 us
  other arithmetic: 26.5 us -> 10.9 us
    unnamed x1 -> x0, blocking collectives: 684 us -> none
    pallas_call x0 -> x5, Pallas kernels: none -> 519 us  [the longest x2 480 us: pack(): pl.pallas_call(kernel, out_shape=jax.ShapeDtypeStruct((slots,) + arrays[0...]
    all_to_all x2 -> x3, waiting for transfers between devices: 9.26 us -> 160 us  [exchange(): return lax.all_to_all(x, 'shard', split_axis=0, concat_axis=0, tiled=True)]
    gather x4 -> x0, local copies, waits for them, and re-layouts: 37.3 us -> none  [the longest x1 17.9 us: per_device(): query_embedding = embeddings[query_pick]]
    all_gather x0 -> x1, blocking collectives: none -> 37.3 us  [per_device(): plan = lax.all_gather(plan, 'shard', axis=0, tiled=True)]
    dot_general x1 -> x0, matrix products: 31.2 us -> none  [pair_side_flags(): jnp.einsum('dzp,dwp->dzw', query_embedding, partner_embedding, preferred_...]
    all_to_all x2 -> x3, starting transfers between devices: 11 us -> 40.9 us  [exchange(): return lax.all_to_all(x, 'shard', split_axis=0, concat_axis=0, tiled=True)]
    all_to_all x1 -> x0, blocking collectives: 20.9 us -> none  [per_device(): lax.all_to_all(wanted[:, None], 'shard', split_axis=0, concat_axis=0, til...]
  transfers between devices with their start and end apart: 2 -> 4, of which waited for: 1 -> 3; matrix products, arithmetic and copies ran while one was open for 3% -> 4% of each run, Pallas kernels for 0% -> 2%
where the time goes in v1:
time: 801 us; the launch traced here: 798 us
  Pallas kernels  519 us (65%)
  waiting for transfers between devices  160 us (20%)
  starting transfers between devices  42.4 us (5%)
  blocking collectives  37.3 us (5%)
  matrix products  19.2 us (2%)
  other arithmetic  10.9 us (1%)
    pallas_call x2, Pallas kernels, pack(): pl.pallas_call(kernel, out_shape=jax.ShapeDtypeStruct((slots,) + arrays[0...  480 us
    all_to_all x3, waiting for transfers between devices, exchange(): return lax.all_to_all(x, 'shard', split_axis=0, concat_axis=0, tiled=True)  160 us
    all_to_all x3, starting transfers between devices, exchange(): return lax.all_to_all(x, 'shard', split_axis=0, concat_axis=0, tiled=True)  40.9 us
    all_gather x1, blocking collectives, per_device(): plan = lax.all_gather(plan, 'shard', axis=0, tiled=True)  37.3 us
    pallas_call x1, Pallas kernels, match(): pl.pallas_call(functools.partial(match_kernel, n1), out_shape=[jax.ShapeD...  23.5 us
    dot_general x2, matrix products, one_block(): jnp.einsum('bie,qje->bqij', block_rows, embeddings, preferred_element_typ...  19.2 us
  transfers between devices with their start and end apart: 4, of which 3 were waited for; matrix products, arithmetic and copies ran while one was open for 4% of the time, Pallas kernels for 2%

profile of v1, /device:TPU:1, one launch (start us, length us, event | category | flops | bytes accessed | tf_op | source)
XLA Modules:
  0.0 797.8 jit_solution(6412023037110459252)
XLA Ops:
  0.6 1.5 collective-permute-start
  2.1 0.7 add_bitcast_fusion
  2.8 37.3 %all-gather = s32[128,1,272]{2,1,0:T(1,128)S(1)} all-gather(s32[1,1,272]{2,1,0:T(1,128)S(1)} %add_bitcast_fusion), channel_id=1, replica_groups=mesh['shard'=128] {'shard'}, dimensions={0}, use_global_device_ids=true | all-gather | bytes 140352 | tf_op jit(solution)/shard_map/all_gather | solution.py:413
  40.5 10.5 %route1.1 = s32[16,128]{1,0:T(8,128)S(1)} custom-call(s32[1]{0:T(128)} %bitcast.44.me_ref, s32[128,128]{1,0:T(8,128)S(1)} %copy.56.req_ref, s32[128,128]{1,0:T(8,128)S(1)} %copy.57.q_ref, s32[128,16]{1,0:T(8,128)S(1)} %copy.58.lens_ref, s32[16,128]{1,0:T(8,128)S(1)} %get-tuple-element.440.lens_t_ref), custom_call_target="tpu_custom_call" | custom-call | tf_op jit(solution)/shard_map/route1/pallas_call | solution.py:148
  52.3 0.7 fusion.30
  53.0 744.8 %conditional.2 = (f32[16,128]{1,0:T(8,128)}, f32[16,128]{1,0:T(8,128)}) conditional(s32[]{:T(128)} %bitcast.49, (s32[128,16]{0,1:T(8,128)S(1)}, s32[1]{0:T(128)}, s32[128,128]{0,1:T(8,128)S(1)}, s32[128,128]{0,1:T(8,128)S(1)}, f32[16,128]{0,1:T(8,128)S(1)}, /*index=5*/bf16[16,128,1280]{2,1,0:T(8,128)(2,1)}, bf16[128,16,1280]{2,1,0:T(8,128)(2,1)}, ...), branch_computations={%region_0.23_spmd, %region_23.34_spmd} | conditional | flops 5390275584 | bytes 151897680 | solution.py:449
  53.2 319.6 %branch_1_fun.9 = bf16[256,16,1280]{2,1,0:T(8,128)(2,1)} custom-call(s32[16,128]{1,0:T(8,128)} %get-tuple-element.241.tab_ref, bf16[128,16,1280]{2,1,0:T(8,128)(2,1)} %bitcast.173, bf16[128,16,1280]{2,1,0:T(8,128)(2,1)} %get-tuple-element.243.mate_ref), custom_call_target="tpu_custom_call" | custom-call | tf_op jit(solution)/shard_map/cond/branch_1_fun/pallas_call | solution.py:223
  372.8 5.9 all-to-all-start
  378.9 33.6 %while.32 = (s32[]{:T(128)}, f32[2,8,128]{2,1,0:T(8,128)S(1)}, s32[2]{0:T(128)S(1)}, f32[16,128]{1,0:T(8,128)S(1)}, bf16[16,128,1280]{2,1,0:T(8,128)(2,1)}, /*in...) while((s32[]{:T(128)}, f32[2,8,128]{2,1,0:T(8,128)S(1)}, s32[2]{0:T(128)S(1)}, ...), condition=%wide.region_32.32_spmd, body=%wide.region_25.0_spmd.sunk | while | flops 5389736960 | bytes 25377404 | solution.py:400
  381.6 10.0 %multiply_reduce_fusion.15 = (f32[8,16,128]{2,1,0:T(8,128)S(1)}, f32[8,128,16]{1,2,0:T(8,128)S(1)}, f32[8,128,16,128]{1,3,2,0:T(8,128)S(1)}) fusion(f32[8,128]{1,0:T(8,128)S(1)} %broadcast_multiply_fusion.12, f32[16,128]{1,0:T(8,128)S(1)} %broadcast_multiply_fusion.13, bf16[16,128,1280]{2,1,0:T(8,128)(2,1)} %get-tuple-element.625, s32[]{:T(128)S(6)} %select_n.110), kind=kOutput, calls=%fused_computation.69.clone.1 | convolution fusion | flops 5377064960 | bytes 16396292 | tf_op jit(solution)/shard_map/cond/branch_1_fun/while/body/eval_jaxpr/bie,qje->bqij/dot_general | solution.py:387
  391.8 3.4 fusion.42
  395.2 0.7 iota_add_fusion.6
  398.7 9.3 %multiply_reduce_fusion.15 = (f32[8,16,128]{2,1,0:T(8,128)S(1)}, f32[8,128,16]{1,2,0:T(8,128)S(1)}, f32[8,128,16,128]{1,3,2,0:T(8,128)S(1)}) fusion(f32[8,128]{1,0:T(8,128)S(1)} %broadcast_multiply_fusion.12, f32[16,128]{1,0:T(8,128)S(1)} %broadcast_multiply_fusion.13, bf16[16,128,1280]{2,1,0:T(8,128)(2,1)} %get-tuple-element.625, s32[]{:T(128)S(6)} %select_n.110), kind=kOutput, calls=%fused_computation.69.clone.1 | convolution fusion | flops 5377064960 | bytes 16396292 | tf_op jit(solution)/shard_map/cond/branch_1_fun/while/body/eval_jaxpr/bie,qje->bqij/dot_general | solution.py:387
  408.3 3.4 fusion.42
  412.5 90.6 %all-to-all-done.got_ref.got1_ref = bf16[256,16,1280]{2,1,0:T(8,128)(2,1)} async-done(((bf16[256,16,1280]{2,1,0:T(8,128)(2,1)}), bf16[256,16,1280]{2,1,0:T(8,128)(2,1)}, u32[]{:S(2)}, u32[]{:S(2)}) %all-to-all-start) | async-done | bytes 10485792 | tf_op jit(solution)/shard_map/cond/branch_1_fun/all_to_all | solution.py:404
  503.1 160.6 %branch_1_fun.11 = bf16[128,16,1280]{2,1,0:T(8,128)(2,1)} custom-call(s32[16,128]{1,0:T(8,128)S(1)} %copy-done.4, bf16[128,16,1280]{2,1,0:T(8,128)(2,1)} %bitcast.174, bf16[128,16,1280]{2,1,0:T(8,128)(2,1)} %get-tuple-element.243.mate_ref, bf16[256,16,1280]{2,1,0:T(8,128)(2,1)} %all-to-all-done.got_ref.got1_ref), custom_call_target="tpu_custom_call" | custom-call | tf_op jit(solution)/shard_map/cond/branch_1_fun/pallas_call | solution.py:223
  663.7 9.1 %all-to-all-start.1 = ((bf16[128,16,1280]{2,1,0:T(8,128)(2,1)}), bf16[128,16,1280]{2,1,0:T(8,128)(2,1)}, u32[]{:S(2)}, u32[]{:S(2)}) async-start(bf16[128,16,1280]{2,1,0:T(8,128)(2,1)} %branch_1_fun.11), calls=%async_computation.1 | async-start | bytes 10485760 | tf_op jit(solution)/shard_map/cond/branch_1_fun/all_to_all | solution.py:404
  672.8 4.6 branch_1_fun.10.loc_ref
  677.4 59.5 %all-to-all-done.1.got2_ref = bf16[128,16,1280]{2,1,0:T(8,128)(2,1)} async-done(((bf16[128,16,1280]{2,1,0:T(8,128)(2,1)}), bf16[128,16,1280]{2,1,0:T(8,128)(2,1)}, u32[]{:S(2)}, u32[]{:S(2)}) %all-to-all-start.1) | async-done | bytes 5242912 | tf_op jit(solution)/shard_map/cond/branch_1_fun/all_to_all | solution.py:404
  736.9 0.7 copy-done.2
  737.6 23.5 %match.5 = (f32[128,128]{1,0:T(8,128)S(1)}, f32[128,128]{1,0:T(8,128)}) custom-call(s32[16,128]{1,0:T(8,128)S(1)} %copy-done.4, s32[1280]{0:T(1024)S(1)} %copy-done.2, s32[16]{0:T(128)S(1)} %copy-done.7, bf16[16,128,1280]{2,1,0:T(8,128)(2,1)} %get-tuple-element.694, bf16[256,16,1280]{2,1,0:T(8,128)(2,1)} %all-to-all-done.got_ref.got1_ref, ...), custom_call_target="tpu_custom_call" | custom-call | tf_op jit(solution)/shard_map/cond/branch_1_fun/match/pallas_call | solution.py:350
  761.2 25.9 %all-to-all-start.2 = ((f32[128,1,128]{2,1,0:T(1,128)}), f32[128,1,128]{2,1,0:T(1,128)S(1)}, u32[]{:S(2)}, u32[]{:S(2)}) async-start(f32[128,1,128]{2,1,0:T(1,128)} %bitcast.41), calls=%async_computation.2 | async-start | bytes 131072 | tf_op jit(solution)/shard_map/cond/branch_1_fun/all_to_all | solution.py:404
  787.1 9.6 %all-to-all-done.2 = f32[128,1,128]{2,1,0:T(1,128)S(1)} async-done(((f32[128,1,128]{2,1,0:T(1,128)}), f32[128,1,128]{2,1,0:T(1,128)S(1)}, u32[]{:S(2)}, u32[]{:S(2)}) %all-to-all-start.2) | async-done | bytes 65568 | tf_op jit(solution)/shard_map/cond/branch_1_fun/all_to_all | solution.py:404
  797.1 0.7 copy.66
  (48 shorter events, 4.5 us)
Async XLA Ops:
  0.6 52.3 %collective-permute-start = (bf16[16,128,1280]{2,1,0:T(8,128)(2,1)}, bf16[16,128,1280]{2,1,0:T(8,128)(2,1)}, u32[]{:S(2)}, u32[]{:S(2)}) collective-permute-start(bf16[16,128,1280]{2,1,0:T(8,128)(2,1)} %param.14), channel_id=1, source_target_pairs={{0,1},{1,0},{2,3},{3,2},{4,5},{5,4},{6,7},{7,6},{8,9},{9,8},{10,11... | collective-permute-start | bytes 15728648 | tf_op jit(solution)/shard_map/ppermute | solution.py:411
  51.1 1.2 copy-start.3
  372.8 130.2 %all-to-all-start = ((bf16[256,16,1280]{2,1,0:T(8,128)(2,1)}), bf16[256,16,1280]{2,1,0:T(8,128)(2,1)}, u32[]{:S(2)}, u32[]{:S(2)}) async-start(bf16[256,16,1280]{2,1,0:T(8,128)(2,1)} %branch_1_fun.9), calls=%async_computation | async-start | bytes 20971520 | tf_op jit(solution)/shard_map/cond/branch_1_fun/all_to_all | solution.py:404
  378.9 124.2 %copy-start.4 = (s32[16,128]{1,0:T(8,128)S(1)}, s32[16,128]{1,0:T(8,128)}, u32[]{:S(2)}) copy-start(s32[16,128]{1,0:T(8,128)} %get-tuple-element.241.tab_ref) | copy-start | bytes 24580 | tf_op jit(solution)/shard_map/cond
  412.5 251.2 %copy-start.11 = (f32[2,8,128]{2,1,0:T(8,128)}, f32[2,8,128]{2,1,0:T(8,128)S(1)}, u32[]{:S(2)}) copy-start(f32[2,8,128]{2,1,0:T(8,128)S(1)} %get-tuple-element.246) | copy-start | bytes 24580 | tf_op jit(solution)/shard_map/cond
  663.7 73.2 %copy-start.7 = (s32[16]{0:T(128)S(1)}, s32[16]{0:T(128)}, u32[]{:S(2)}) copy-start(s32[16]{0:T(128)} %get-tuple-element.249.lens_ref) | copy-start | bytes 196 | tf_op jit(solution)/shard_map/cond
  663.7 73.2 %all-to-all-start.1 = ((bf16[128,16,1280]{2,1,0:T(8,128)(2,1)}), bf16[128,16,1280]{2,1,0:T(8,128)(2,1)}, u32[]{:S(2)}, u32[]{:S(2)}) async-start(bf16[128,16,1280]{2,1,0:T(8,128)(2,1)} %branch_1_fun.11), calls=%async_computation.1 | async-start | bytes 10485760 | tf_op jit(solution)/shard_map/cond/branch_1_fun/all_to_all | solution.py:404
  736.9 0.7 copy-start.2
  761.2 35.5 %all-to-all-start.2 = ((f32[128,1,128]{2,1,0:T(1,128)}), f32[128,1,128]{2,1,0:T(1,128)S(1)}, u32[]{:S(2)}, u32[]{:S(2)}) async-start(f32[128,1,128]{2,1,0:T(1,128)} %bitcast.41), calls=%async_computation.2 | async-start | bytes 131072 | tf_op jit(solution)/shard_map/cond/branch_1_fun/all_to_all | solution.py:404
